TPU v7x, 32 devices: a whole 2x2x4 slice. The times are simulated.
32 devices in a mesh: tm: 4 (over z), queue: 8 (over y, x, core).
Axes of the slice: x: 2, y: 2, z: 4, core: 2. Of those that a mesh axis runs over, the one named last changes fastest.
Arguments:
- clips: bfloat16 [8192, 512], P('tm'), may hold values from -6 to 6
- narrations: bfloat16 [8192, 512], P('tm'), may hold values from -6 to 6
- queue: bfloat16 [8192, 512], P('queue'), may hold values from -6 to 6
- loss_weights: float32 [8192], P('tm'), may hold values from 0.5 to 4
- offsets: int32 [8192, 8], P('tm'), may hold values from -4 to 4
- valid: int32 [8192, 8], P('tm'), may hold values 0 or 1
Outputs:
- grad_clips: bfloat16 [8192, 512], P(('tm', 'queue'))
- grad_narrations: bfloat16 [8192, 512], P('tm')
- grad_queue: bfloat16 [8192, 512], P('queue')
All inputs are finite; a program needn't handle non-finite values. No bound on the sum of `valid` on one device may be relied on, other than what follows from the above.
Results may differ from a plain program's by a relative error of at most 0.0051.
Values may be sent and summed in bfloat16 or wider, within the bound.
A program may use at most 192 MiB of HBM per device.

v0:
```python
import math

import jax
import jax.numpy as jnp
from jax import lax
from jax.sharding import PartitionSpec as P

HALO = 4


def with_halo(array, sides, width):
    for axis, dim in sides:
        devices, length = (lax.axis_size(axis), array.shape[dim])
        up = [(i, (i + 1) % devices) for i in range(devices - 1)]
        down = [(j, i) for i, j in up]
        last = lax.slice_in_dim(array, length - width, length, axis=dim)
        leading = lax.slice_in_dim(array, 0, width, axis=dim)
        before = lax.ppermute(last, axis, up)
        after = lax.ppermute(leading, axis, down)
        array = jnp.concatenate([before, array, after], axis=dim)
    return array


def shifted(value, axis, steps):
    count = lax.axis_size(axis)
    leading, last = (max(0, -steps), min(count, count - steps))
    return lax.ppermute(value, axis, [(source, source + steps) for source in range(leading, last)])


def shards(clips, narrations, queue, loss_weights, offsets, valid):
    rows, width = clips.shape
    scale = 0.75 / math.sqrt(width)
    total_clips = rows * lax.axis_size("tm")
    position = lax.axis_index("tm") * rows + jnp.arange(rows, dtype=jnp.int32)
    extended = with_halo(narrations, (("tm", 0),), HALO)
    valid_f = valid.astype(jnp.float32)
    score_list = []
    count_list = []
    for delta in range(-HALO, HALO + 1):
        piece = extended[HALO + delta : HALO + delta + rows]
        score_list.append(
            scale * jnp.einsum("ie,ie->i", clips, piece, preferred_element_type=jnp.float32)
        )
        inside = ((position + delta >= 0) & (position + delta < total_clips)).astype(jnp.float32)
        hits = jnp.sum(valid_f * (offsets == delta).astype(jnp.float32), axis=1)
        own = 1.0 if delta == 0 else 0.0
        count_list.append((own + hits) * inside)
    bag_scores = jnp.stack(score_list)
    counts = jnp.stack(count_list)
    bag_top = jnp.max(jnp.where(counts > 0, bag_scores, -jnp.inf), axis=0)
    bag_sum = jnp.sum(counts * jnp.exp(bag_scores - bag_top[None, :]), axis=0)
    scores = scale * lax.dot_general(
        clips, queue, (((1,), (1,)), ((), ())), preferred_element_type=jnp.float32
    )
    local_top = jnp.maximum(jnp.max(scores, axis=1), bag_top)
    shift = lax.pmax(local_top, "queue")
    expo = jnp.exp(scores - shift[:, None])
    negative = lax.psum(jnp.sum(expo, axis=1), "queue")
    bag_part = bag_sum * jnp.exp(bag_top - shift)
    total = negative + bag_part
    share = bag_part / total
    neg_coef = ((loss_weights / total)[:, None] * expo).astype(jnp.bfloat16)
    bag_coef = (
        loss_weights[None, :]
        * counts
        * jnp.exp(bag_scores - bag_top[None, :])
        / bag_sum[None, :]
        * (share[None, :] - 1.0)
    ).astype(jnp.bfloat16)
    bag_grad = jnp.zeros((rows, width), jnp.float32)
    narr_grad = jnp.zeros((rows + 2 * HALO, width), jnp.float32)
    for slot, delta in enumerate(range(-HALO, HALO + 1)):
        coef = bag_coef[slot].astype(jnp.float32)[:, None]
        bag_grad = bag_grad + coef * extended[HALO + delta : HALO + delta + rows]
        narr_grad = narr_grad + jnp.pad(coef * clips, ((HALO + delta, HALO - delta), (0, 0)))
    own_rows = rows // lax.axis_size("queue")
    own_start = lax.axis_index("queue") * own_rows
    summed = lax.psum(jnp.dot(neg_coef, queue, preferred_element_type=jnp.float32), "queue")
    neg_grad = lax.dynamic_slice_in_dim(summed, own_start, own_rows, 0)
    own_bag = lax.dynamic_slice_in_dim(bag_grad, own_start, own_rows, 0)
    grad_clips = (scale * (own_bag + neg_grad)).astype(jnp.bfloat16)
    from_next = shifted(narr_grad[:HALO], "tm", -1)
    from_prev = shifted(narr_grad[-HALO:], "tm", 1)
    middle = narr_grad[HALO : HALO + rows]
    middle = jnp.concatenate(
        [middle[:HALO] + from_prev, middle[HALO : rows - HALO], middle[rows - HALO :] + from_next],
        axis=0,
    )
    grad_narrations = (scale * middle).astype(jnp.bfloat16)
    partial_q = lax.dot_general(
        neg_coef, clips, (((0,), (0,)), ((), ())), preferred_element_type=jnp.float32
    )
    grad_queue = (scale * lax.psum(partial_q, "tm")).astype(jnp.bfloat16)
    return (grad_clips, grad_narrations, grad_queue)


def solution(mesh):
    placed = (P("tm", None), P("tm", None), P("queue", None), P("tm"), P("tm", None), P("tm", None))
    return jax.shard_map(
        shards,
        mesh=mesh,
        in_specs=placed,
        out_specs=(P(("tm", "queue"), None), P("tm", None), P("queue", None)),
        check_vma=False,
    )
```

profile of v0, /device:TPU:24, one launch (start us, length us, event | category | flops | bytes accessed | tf_op | source)
XLA Modules:
  0.0 256.0 jit_solution(15408431023409609083)
XLA Ops:
  7.2 0.8 fusion.27
  8.0 2.3 collective-permute-start.1
  10.4 1.4 collective-permute-start
  11.8 4.8 %fusion.28 = (f32[2048,512]{1,0:T(8,128)}, bf16[2052,512]{1,0:T(8,128)(2,1)S(1)}) fusion(bf16[2048,512]{1,0:T(8,128)(2,1)} %param.7), kind=kLoop, calls=%fused_computation.119 | loop fusion | flops 1048575 | bytes 8388608
  16.7 0.2 select_reduce_fusion.1
  17.1 7.2 %multiply_reduce_fusion = (f32[2048]{0:T(1024)S(1)}, f32[2048,1024]{0,1:T(8,128)}) fusion(bf16[2048,512]{1,0:T(8,128)(2,1)} %param.6, bf16[1024,512]{1,0:T(8,128)(2,1)S(1)} %copy-done), kind=kOutput, calls=%fused_computation.20 | convolution fusion | flops 2151675904 | bytes 11542528 | tf_op jit(solution)/shard_map/dot_general | solution.py:52
  24.3 0.1 stack.42
  24.4 12.5 %fusion.10 = (f32[2048]{0:T(1024)S(1)}, f32[2048]{0:T(1024)S(1)}, f32[2048]{0:T(1024)S(1)}, f32[2048]{0:T(1024)S(1)}, f32[2048]{0:T(1024)S(1)}, /*index=5*/f32[2...) fusion(bf16[2048,512]{1,0:T(8,128)(2,1)} %param.6, ...), kind=kLoop, calls=%fused_computation.36 | loop fusion | flops 41924608 | bytes 12660736 | tf_op jit(solution)/shard_map/ie,ie->i/dot_general | solution.py:42
  37.0 0.1 stack.52
  37.2 13.6 %pmax.7 = f32[2048]{0:T(1024)S(1)} all-reduce(f32[2048]{0:T(1024)S(1)} %max.5), channel_id=1, replica_groups=mesh['tm'=4,'queue'=8] {'queue'}, use_global_device_ids=true, to_apply=%region_12.13 | all-reduce | flops 2048 | bytes 16384 | tf_op jit(solution)/shard_map/pmax | solution.py:56
  50.9 4.8 %fusion = f32[2048]{0:T(1024)S(1)} fusion(f32[2048,1024]{0,1:T(8,128)} %get-tuple-element.61, f32[2048]{0:T(1024)S(1)} %pmax.7), kind=kLoop, calls=%fused_computation.21 | loop fusion | flops 6289408 | bytes 8404992 | tf_op jit(solution)/shard_map/reduce_sum | solution.py:58
  55.7 12.1 %psum.21 = f32[2048]{0:T(1024)S(1)} all-reduce(f32[2048]{0:T(1024)S(1)} %fusion), channel_id=1, replica_groups=mesh['tm'=4,'queue'=8] {'queue'}, use_global_device_ids=true, to_apply=%region_14.15 | all-reduce | flops 2048 | bytes 16384 | tf_op jit(solution)/shard_map/psum | solution.py:58
  68.0 7.7 %fusion.23 = f32[1024,512]{1,0:T(8,128)} fusion(bf16[2048,512]{1,0:T(8,128)(2,1)} %param.6, f32[2048,1024]{0,1:T(8,128)} %get-tuple-element.61, f32[2048]{0:T(1024)S(1)} %get-tuple-element.58, f32[2048]{0:T(1024)S(1)} %pmax.7), kind=kOutput, calls=%fused_computation.69 | convolution fusion | flops 2155872256 | bytes 12599296 | tf_op jit(solution)/shard_map/dot_general | solution.py:90
  75.7 0.2 all-reduce.12.cloned.1.call-start
  75.9 18.8 %convert_multiply_fusion.9 = (f32[2048,512]{1,0:T(8,128)S(1)}, f32[2048,512]{1,0:T(8,128)}, f32[2048,512]{1,0:T(8,128)}, f32[2048,512]{1,0:T(8,128)}, f32[2048,5...) fusion(bf16[2048,512]{1,0:T(8,128)(2,1)} %param.6, ...), kind=kLoop, calls=%fused_computation.9 | loop fusion | flops 33554432 | bytes 50409472 | tf_op jit(solution)/shard_map/mul | solution.py:75
  94.7 12.4 %pad_add_fusion = f32[2056,512]{1,0:T(8,128)S(1)} fusion(f32[2048,512]{1,0:T(8,128)} %get-tuple-element.42, f32[2048,512]{1,0:T(8,128)} %get-tuple-element.41, f32[2048,512]{1,0:T(8,128)} %get-tuple-element.40, f32[2048,512]{1,0:T(8,128)} %get-tuple-element.39, f32[2048,512]{1,0:T(8,128)} %get-tuple-element.38, f32[2048,512]{1,0:T(8,128)} %get-tuple-element.37, ...), kind=kLoop, calls=%fused_computation.26 | loop fusion | flops 8421376 | bytes 41959424 | tf_op jit(solution)/shard_map/add | solution.py:75
  107.1 1.9 copy-done.1
  109.0 4.2 %collective-permute-start.3 = (f32[4,512]{1,0:T(4,128)S(1)}, f32[4,512]{1,0:T(4,128)S(1)}, u32[]{:S(2)}, u32[]{:S(2)}) collective-permute-start(f32[4,512]{1,0:T(4,128)S(1)} %slice.139), channel_id=1, source_target_pairs={{8,0},{16,8},{24,16},{9,1},{17,9},{25,17},{10,2},{18,10},{26,18},{... | collective-permute-start | bytes 24584 | tf_op jit(solution)/shard_map/ppermute | solution.py:27
  113.2 7.8 %fusion.24 = f32[2048,512]{1,0:T(8,128)} fusion(bf16[1024,512]{1,0:T(8,128)(2,1)S(1)} %copy-done, f32[2048,1024]{0,1:T(8,128)} %get-tuple-element.61, f32[2048]{0:T(1024)S(1)} %get-tuple-element.58, f32[2048]{0:T(1024)S(1)} %pmax.7), kind=kOutput, calls=%fused_computation.70 | convolution fusion | flops 2155872256 | bytes 13647872 | tf_op jit(solution)/shard_map/dot_general | solution.py:78
  121.0 0.8 slice_add_fusion
  121.9 1.3 collective-permute-start.2
  123.1 6.9 %slice_convert_fusion.3 = (f32[2048,512]{1,0:T(8,128)}, f32[2048,512]{1,0:T(8,128)}, f32[2048,512]{1,0:T(8,128)}, f32[2048,512]{1,0:T(8,128)}) fusion(bf16[2052,512]{1,0:T(8,128)(2,1)S(1)} %constant_dynamic-update-slice_fusion), kind=kLoop, calls=%fused_computation.48 | loop fusion | flops 4194304 | bytes 25165824
  130.1 4.6 %slice.137 = f32[2040,512]{1,0:T(8,128)} slice(f32[2056,512]{1,0:T(8,128)} %copy-done.1), slice={[8:2048], [0:512]} | slice | bytes 8355840 | tf_op jit(solution)/shard_map/slice | solution.py:86
  134.9 0.1 dynamic-slice.3
  135.0 0.1 dynamic-slice.4
  135.0 0.7 slice_add_fusion.1
  135.8 13.4 %concatenate.18 = f32[2048,512]{1,0:T(8,128)} concatenate(f32[4,512]{1,0:T(4,128)S(1)} %slice_add_fusion.1, f32[2040,512]{1,0:T(8,128)} %slice.137, f32[4,512]{1,0:T(4,128)S(1)} %get-tuple-element.26), dimensions={0} | concatenate | bytes 8388608 | tf_op jit(solution)/shard_map/concatenate | solution.py:85
  149.1 4.1 %multiply_convert_fusion.1 = bf16[2048,512]{1,0:T(8,128)(2,1)} fusion(f32[2048,512]{1,0:T(8,128)} %concatenate.18), kind=kLoop, calls=%fused_computation.38 | loop fusion | flops 2097152 | bytes 6291456 | tf_op jit(solution)/shard_map/convert_element_type | solution.py:89
  153.3 7.3 %all-reduce.14.cloned.1.call-done = f32[1024,512]{1,0:T(8,128)} async-done(((f32[1024,512]{1,0:T(8,128)}), f32[1024,512]{1,0:T(8,128)}) %all-reduce.14.cloned.1.call-update) | async-done | bytes 2097168 | tf_op jit(solution)/shard_map/psum | solution.py:93
  160.5 2.8 %multiply_convert_fusion.2 = bf16[1024,512]{1,0:T(8,128)(2,1)} fusion(f32[1024,512]{1,0:T(8,128)} %all-reduce.14.cloned.1.call-done), kind=kLoop, calls=%fused_computation.50 | loop fusion | flops 1048576 | bytes 3145728 | tf_op jit(solution)/shard_map/convert_element_type | solution.py:93
  163.4 82.7 %all-reduce.12.cloned.1.call-done = f32[2048,512]{1,0:T(8,128)} async-done(((f32[2048,512]{1,0:T(8,128)}), f32[2048,512]{1,0:T(8,128)}) %all-reduce.12.cloned.1.call-update) | async-done | bytes 4194320 | tf_op jit(solution)/shard_map/psum | solution.py:78
  246.0 3.2 %fusion.18 = bf16[256,512]{1,0:T(8,128)(2,1)} fusion(f32[2048,512]{1,0:T(8,128)} %get-tuple-element.29, s32[]{:T(128)S(6)} %select_n.9, f32[2048,512]{1,0:T(8,128)} %get-tuple-element.30, f32[2048,512]{1,0:T(8,128)} %get-tuple-element.31, f32[2048,512]{1,0:T(8,128)} %get-tuple-element.28, f32[2048,512]{1,0:T(8,128)} %get-tuple-element.45, ...), kind=kLoop, calls=%fused_computation.55 | loop fusion | flops 1835008 | bytes 4461572 | tf_op jit(solution)/shard_map/convert_element_type | solution.py:81
  (38 shorter events, 0.7 us)
Async XLA Ops:
  7.2 9.9 %copy-start = (bf16[1024,512]{1,0:T(8,128)(2,1)S(1)}, bf16[1024,512]{1,0:T(8,128)(2,1)}, u32[]{:S(2)}) copy-start(bf16[1024,512]{1,0:T(8,128)(2,1)} %param.8) | copy-start | bytes 3145732
  7.2 153.3 %all-reduce.14.cloned.1.call-start = ((), (), s32[]{:S(2)}) async-start(), calls=%async_computation.1 | async-start | bytes 4194304 | tf_op jit(solution)/shard_map/psum | solution.py:93
  8.0 16.4 %collective-permute-start.1 = (bf16[4,512]{1,0:T(4,128)(2,1)S(1)}, bf16[4,512]{1,0:T(4,128)(2,1)S(1)}, u32[]{:S(2)}, u32[]{:S(2)}) collective-permute-start(bf16[4,512]{1,0:T(4,128)(2,1)S(1)} %get-tuple-element.44), channel_id=1, source_target_pairs={{8,0},{16,8},{24,16},{9,1},{17,9},{25,17},{10,2},{18,10},{26,18},{... | collective-permute-start | bytes 12296 | tf_op jit(solution)/shard_map/ppermute | solution.py:19
  10.4 6.3 %copy-start.2 = (s32[2048,8]{0,1:T(8,128)S(1)}, s32[2048,8]{0,1:T(8,128)}, u32[]{:S(2)}) copy-start(s32[2048,8]{0,1:T(8,128)} %param.11) | copy-start | bytes 196612
  10.4 6.3 %copy-start.3 = (s32[2048,8]{0,1:T(8,128)S(1)}, s32[2048,8]{0,1:T(8,128)}, u32[]{:S(2)}) copy-start(s32[2048,8]{0,1:T(8,128)} %param.10) | copy-start | bytes 196612
  10.4 14.0 %collective-permute-start = (bf16[4,512]{1,0:T(4,128)(2,1)S(1)}, bf16[4,512]{1,0:T(4,128)(2,1)S(1)}, u32[]{:S(2)}, u32[]{:S(2)}) collective-permute-start(bf16[4,512]{1,0:T(4,128)(2,1)S(1)} %get-tuple-element.43), channel_id=1, source_target_pairs={{0,8},{8,16},{16,24},{1,9},{9,17},{17,25},{2,10},{10,18},{18,26},{... | collective-permute-start | bytes 12296 | tf_op jit(solution)/shard_map/ppermute | solution.py:18
  50.9 16.9 %copy-start.4 = (f32[2048]{0:T(1024)S(1)}, f32[2048]{0:T(1024)}, u32[]{:S(2)}) copy-start(f32[2048]{0:T(1024)} %param.9) | copy-start | bytes 24580
  75.7 170.4 %all-reduce.12.cloned.1.call-start = ((), (), s32[]{:S(2)}) async-start(), calls=%async_computation | async-start | bytes 8388608 | tf_op jit(solution)/shard_map/psum | solution.py:78
  107.1 1.9 copy-start.1
  109.0 12.0 %collective-permute-start.3 = (f32[4,512]{1,0:T(4,128)S(1)}, f32[4,512]{1,0:T(4,128)S(1)}, u32[]{:S(2)}, u32[]{:S(2)}) collective-permute-start(f32[4,512]{1,0:T(4,128)S(1)} %slice.139), channel_id=1, source_target_pairs={{8,0},{16,8},{24,16},{9,1},{17,9},{25,17},{10,2},{18,10},{26,18},{... | collective-permute-start | bytes 24584 | tf_op jit(solution)/shard_map/ppermute | solution.py:27
  121.9 13.2 %collective-permute-start.2 = (f32[4,512]{1,0:T(4,128)S(1)}, f32[4,512]{1,0:T(4,128)S(1)}, u32[]{:S(2)}, u32[]{:S(2)}) collective-permute-start(f32[4,512]{1,0:T(4,128)S(1)} %get-tuple-element.27), channel_id=1, source_target_pairs={{0,8},{8,16},{16,24},{1,9},{9,17},{17,25},{2,10},{10,18},{18,26},{... | collective-permute-start | bytes 24584 | tf_op jit(solution)/shard_map/ppermute | solution.py:27
Sparse Core Ops, SparseCore 0:
  75.8 84.6 all-reduce.13
  164.1 81.8 all-reduce.11
where the time goes:
time: 259 us; the launch traced here: 256 us
  waiting for transfers between devices  90 us (35%)
  other arithmetic  72.4 us (28%)
  blocking collectives  25.8 us (10%)
  matrix products  22.6 us (9%)
  local copies, waits for them, and re-layouts  21.3 us (8%)
  between operations  14.3 us (6%)
  starting transfers between devices  9.53 us (4%)
    psum x1, waiting for transfers between devices, shards(): lax.psum(jnp.dot(neg_coef, queue, preferred_element_type=jnp.float32), 'q...  82.7 us
    mul x1, other arithmetic, shards(): coef * clips  18.8 us
    pmax x1, blocking collectives, shards(): shift = lax.pmax(local_top, 'queue')  13.6 us
    concatenate x1, local copies, waits for them, and re-layouts, shards(): jnp.concatenate([middle[:HALO] + from_prev, middle[HALO:rows - HALO], mid...  13.4 us
    dot_general x1, other arithmetic, shards(): jnp.einsum('ie,ie->i', clips, piece, preferred_element_type=jnp.float32)  12.5 us
    add x1, other arithmetic, shards(): narr_grad + jnp.pad(coef * clips, ((HALO + delta, HALO - delta), (0, 0)))  12.4 us
    psum x1, blocking collectives, shards(): negative = lax.psum(jnp.sum(expo, axis=1), 'queue')  12.1 us
    unnamed x2, other arithmetic  11.8 us
  transfers between devices with their start and end apart: 6, of which 2 were waited for; matrix products, arithmetic and copies ran while one was open for 33% of the time, Pallas kernels for 0%

commit v1 on v0

v1 whole, which is shorter than its diff:
```python
import functools
import math

import jax
import jax.numpy as jnp
from jax import lax
from jax.experimental import pallas as pl
from jax.experimental.pallas import tpu as pltpu
from jax.sharding import PartitionSpec as P

HALO = 4
PAD = 16
BLK = 128
WIN = BLK + 2 * PAD
LAG = 2
MESH = pl.DeviceIdType.MESH
F32 = jnp.float32
BF16 = jnp.bfloat16
NT = (((1,), (1,)), ((), ()))
TN = (((0,), (0,)), ((), ()))


def dot(a, b, dims=(((1,), (0,)), ((), ()))):
    return lax.dot_general(a, b, dims, preferred_element_type=F32)


def kernel(T, Q, ZC, clips, narr_hbm, queue, weights, offsets, valid, gc_hbm, gn_hbm, gq_hbm,
           ext, scores, coef, stat, bag_s, counts, bag_c, narr_acc, edge, part, up_tx, up_rx, fin,
           grad_f, grad_b, pair_rx, chip_tx, chip_rx, bag_grad, gc_out, gn_out,
           load_sem, halo_ss, halo_rs, stat_ss, stat_rs, up_ss, up_rs, down_ss, down_rs,
           pair_ss, pair_rs, chip_ss, chip_rs, edge_ss, edge_rs, gq_sem, out_sem):
    rows, width = clips.shape
    negs = queue.shape[0]
    scale = 0.75 / math.sqrt(width)
    chips = Q // 2
    own = rows // Q
    zn = negs // ZC
    blocks = rows // BLK
    root = (T - 1) // 2
    t = lax.axis_index("tm")
    q = lax.axis_index("queue")
    chip = q // 2
    core = lax.rem(q, 2)
    has_prev = t > 0
    has_next = t < T - 1

    def remote(src, dst, ss, rs, dev):
        return pltpu.make_async_remote_copy(
            src_ref=src, dst_ref=dst, send_sem=ss, recv_sem=rs, device_id=dev, device_id_type=MESH)

    barrier = pltpu.get_barrier_semaphore()
    for k in range(1, Q):
        pl.semaphore_signal(barrier, inc=1, device_id=(t, lax.rem(q + k, Q)), device_id_type=MESH)

    @pl.when(has_prev)
    def _():
        pl.semaphore_signal(barrier, inc=1, device_id=(t - 1, q), device_id_type=MESH)

    @pl.when(has_next)
    def _():
        pl.semaphore_signal(barrier, inc=1, device_id=(t + 1, q), device_id_type=MESH)

    load = pltpu.make_async_copy(narr_hbm, ext.at[pl.ds(PAD, rows)], load_sem)
    load.start()

    SN = 256

    def score_step(k, top):
        r = pl.ds(pl.multiple_of(k * SN, SN), SN)
        s = scale * dot(queue[r, :], clips[...], NT)
        scores[r, :] = s
        return jnp.maximum(top, jnp.max(s, axis=0, keepdims=True))

    top = lax.fori_loop(0, negs // SN, score_step, jnp.full((1, rows), -jnp.inf, F32))

    load.wait()
    pl.semaphore_wait(barrier, Q - 1 + has_prev.astype(jnp.int32) + has_next.astype(jnp.int32))

    def halo_next():
        return remote(ext.at[pl.ds(rows, PAD)], ext.at[pl.ds(0, PAD)],
                      halo_ss.at[0], halo_rs.at[0], (t + 1, q))

    def halo_prev():
        return remote(ext.at[pl.ds(PAD, PAD)], ext.at[pl.ds(PAD + rows, PAD)],
                      halo_ss.at[1], halo_rs.at[1], (t - 1, q))

    @pl.when(has_next)
    def _():
        halo_next().start()

    @pl.when(has_prev)
    def _():
        halo_prev().start()

    EN = 32

    def exp_step(k, total):
        r = pl.ds(pl.multiple_of(k * EN, EN), EN)
        p = jnp.exp(scores[r, :] - top)
        scores[r, :] = p
        return total + jnp.sum(p, axis=0, keepdims=True)

    local_sum = lax.fori_loop(0, negs // EN, exp_step, jnp.zeros((1, rows), F32))
    stat[q, 0:1, :] = top
    stat[q, 1:2, :] = local_sum

    def stat_copy(k):
        peer = lax.rem(q + k, Q)
        return remote(stat.at[q], stat.at[q], stat_ss.at[k], stat_rs.at[k], (t, peer))

    def stat_arrival(k):
        source = lax.rem(q + Q - k, Q)
        return remote(stat.at[source], stat.at[source], stat_ss.at[k], stat_rs.at[k], (t, source))

    for k in range(1, Q):
        stat_copy(k).start()

    @pl.when(has_prev)
    def _():
        halo_next().wait_recv()

    @pl.when(jnp.logical_not(has_prev))
    def _():
        ext[0:PAD, :] = jnp.zeros((PAD, width), BF16)

    @pl.when(has_next)
    def _():
        halo_prev().wait_recv()

    @pl.when(jnp.logical_not(has_next))
    def _():
        ext[PAD + rows:, :] = jnp.zeros((PAD, width), BF16)

    bag_s[...] = jnp.zeros_like(bag_s)
    counts[...] = jnp.zeros_like(counts)
    delta = (lax.broadcasted_iota(jnp.int32, (WIN, BLK), 0)
             - lax.broadcasted_iota(jnp.int32, (WIN, BLK), 1) - PAD)

    def bag_step(b, _):
        i0 = pl.multiple_of(b * BLK, BLK)
        s = scale * dot(ext[pl.ds(i0, WIN), :], clips[pl.ds(i0, BLK), :], NT)
        for d in range(-HALO, HALO + 1):
            bag_s[d + HALO:d + HALO + 1, pl.ds(i0, BLK)] = jnp.sum(
                jnp.where(delta == d, s, 0.0), axis=0, keepdims=True)
        return 0

    lax.fori_loop(0, blocks, bag_step, 0)

    position = t * rows + lax.broadcasted_iota(jnp.int32, (1, rows), 1)
    used = valid[...] > 0
    for d in range(-HALO, HALO + 1):
        hits = jnp.sum(jnp.where(used & (offsets[...] == d), 1.0, 0.0), axis=0, keepdims=True)
        inside = (position + d >= 0) & (position + d < T * rows)
        counts[d + HALO:d + HALO + 1, :] = jnp.where(inside, hits + (1.0 if d == 0 else 0.0), 0.0)
    count = counts[...]
    bag_top = jnp.max(jnp.where(count > 0, bag_s[...], -jnp.inf), axis=0, keepdims=True)
    bag_e = jnp.where(count > 0, count * jnp.exp(bag_s[...] - bag_top), 0.0)
    bag_sum = jnp.sum(bag_e, axis=0, keepdims=True)

    for k in range(1, Q):
        stat_arrival(k).wait_recv()
    shift = bag_top
    for k in range(Q):
        shift = jnp.maximum(shift, stat[k, 0:1, :])
    bag_part = bag_sum * jnp.exp(bag_top - shift)
    total = bag_part
    for k in range(Q):
        total = total + stat[k, 1:2, :] * jnp.exp(stat[k, 0:1, :] - shift)
    share = bag_part / total
    w = weights[...]
    factor = w / total * jnp.exp(top - shift)
    bag_c[...] = (w * bag_e / bag_sum * (share - 1.0)).astype(BF16).astype(F32)

    left_child = has_prev & (t <= root)
    right_child = has_next & (t >= root)
    leaf = jnp.logical_not(left_child | right_child)

    def zrows(c):
        return pl.ds(pl.multiple_of(c * zn, zn), zn)

    def up_right(c):
        return remote(up_tx.at[zrows(c)], up_rx.at[0, zrows(c)], up_ss.at[c], up_rs.at[0, c], (t + 1, q))

    def up_left(c):
        return remote(up_tx.at[zrows(c)], up_rx.at[1, zrows(c)], up_ss.at[c], up_rs.at[1, c], (t - 1, q))

    def down_left(c):
        return remote(fin.at[zrows(c)], fin.at[zrows(c)], down_ss.at[0, c], down_rs.at[c], (t - 1, q))

    def down_right(c):
        return remote(fin.at[zrows(c)], fin.at[zrows(c)], down_ss.at[1, c], down_rs.at[c], (t + 1, q))

    def store_queue(c):
        return pltpu.make_async_copy(fin.at[zrows(c)], gq_hbm.at[zrows(c)], gq_sem.at[c])

    def pass_down(c):
        @pl.when(left_child)
        def _():
            down_left(c).start()

        @pl.when(right_child)
        def _():
            down_right(c).start()

        store_queue(c).start()

    def send_up(c):
        up_tx[zrows(c), :] = part[zrows(c), :].astype(BF16)

        @pl.when(t < root)
        def _():
            up_right(c).start()

        @pl.when(t > root)
        def _():
            up_left(c).start()

    def queue_part(c, _):
        p = (scores[zrows(c), :] * factor).astype(BF16)
        coef[zrows(c), :] = p
        part[zrows(c), :] = dot(p, clips[...])

        @pl.when(leaf)
        def _():
            send_up(c)

        return 0

    lax.fori_loop(0, ZC, queue_part, 0)

    def gather_up(c):
        @pl.when(left_child)
        def _():
            up_right(c).wait_recv()
            part[zrows(c), :] += up_rx[0, zrows(c), :].astype(F32)

        @pl.when(right_child)
        def _():
            up_left(c).wait_recv()
            part[zrows(c), :] += up_rx[1, zrows(c), :].astype(F32)

        @pl.when(t == root)
        def _():
            fin[zrows(c), :] = (scale * part[zrows(c), :]).astype(BF16)
            pass_down(c)

        @pl.when((t != root) & jnp.logical_not(leaf))
        def _():
            send_up(c)

    def take_down(c):
        @pl.when(t != root)
        def _():
            down_left(c).wait_recv()
            pass_down(c)

    def own_rows(index):
        return pl.ds(pl.multiple_of(index * own, own), own)

    def pair_copy(p):
        return remote(grad_b.at[own_rows(2 * p + 1 - core)], pair_rx.at[p],
                      pair_ss.at[p], pair_rs.at[p], (t, q + 1 - 2 * core))

    def pair_part(p, _):
        r = pl.ds(pl.multiple_of(p * 2 * own, 2 * own), 2 * own)
        g = dot(coef[:, r], queue[...], TN)
        grad_f[r, :] = g
        grad_b[r, :] = g.astype(BF16)
        pair_copy(p).start()
        return 0

    lax.fori_loop(0, chips, pair_part, 0)

    def chip_copy(k):
        peer = lax.rem(chip + k, chips)
        return remote(chip_tx.at[peer], chip_rx.at[k], chip_ss.at[k], chip_rs.at[k], (t, 2 * peer + core))

    def chip_part(k):
        p = lax.rem(chip + k, chips)
        pair_copy(p).wait_recv()
        g = grad_f[own_rows(2 * p + core), :] + pair_rx[p].astype(F32)
        if isinstance(k, int) and k == 0:
            grad_f[own_rows(2 * p + core), :] = g
        else:
            chip_tx[p] = g.astype(BF16)
            chip_copy(k).start()

    narr_acc[0:2 * PAD, :] = jnp.zeros((2 * PAD, width), F32)

    def narr_part(b):
        i0 = pl.multiple_of(b * BLK, BLK)
        c = bag_c[:, pl.ds(i0, BLK)]
        band = jnp.zeros((WIN, BLK), F32)
        for d in range(-HALO, HALO + 1):
            band = jnp.where(delta == d, c[d + HALO:d + HALO + 1, :], band)
        band = band.astype(BF16)
        g = dot(band, clips[pl.ds(i0, BLK), :])
        narr_acc[pl.ds(i0, 2 * PAD), :] += g[:2 * PAD]
        narr_acc[pl.ds(i0 + 2 * PAD, BLK), :] = g[2 * PAD:]

        @pl.when((i0 + BLK > q * own) & (i0 < (q + 1) * own))
        def _():
            bag_grad[pl.ds(i0, BLK), :] = dot(band, ext[pl.ds(i0, WIN), :], TN)

    chip_steps = -(-(chips - 1) // ZC)
    narr_steps = -(-blocks // ZC)

    def mixed(c, _):
        gather_up(c)
        for j in range(chip_steps):
            k = c * chip_steps + j + 1

            @pl.when(k < chips)
            def _():
                chip_part(k)

        for j in range(narr_steps):
            b = c * narr_steps + j

            @pl.when(b < blocks)
            def _():
                narr_part(b)

        @pl.when(c >= LAG)
        def _():
            take_down(c - LAG)

        return 0

    lax.fori_loop(0, ZC, mixed, 0)

    def edge_next():
        return remote(narr_acc.at[pl.ds(PAD + rows, PAD)], edge.at[0], edge_ss.at[0], edge_rs.at[0], (t + 1, q))

    def edge_prev():
        return remote(narr_acc.at[pl.ds(0, PAD)], edge.at[1], edge_ss.at[1], edge_rs.at[1], (t - 1, q))

    @pl.when(has_next)
    def _():
        edge_next().start()

    @pl.when(has_prev)
    def _():
        edge_prev().start()

    chip_part(0)
    g = grad_f[own_rows(q), :] + bag_grad[own_rows(q), :]
    for k in range(1, chips):
        chip_copy(k).wait_recv()
        g = g + chip_rx[k].astype(F32)
    gc_out[...] = (scale * g).astype(BF16)
    clips_store = pltpu.make_async_copy(gc_out, gc_hbm, out_sem.at[0])
    clips_store.start()

    @pl.when(has_prev)
    def _():
        edge_next().wait_recv()
        narr_acc[PAD:2 * PAD, :] += edge[0]

    @pl.when(has_next)
    def _():
        edge_prev().wait_recv()
        narr_acc[rows:rows + PAD, :] += edge[1]

    def narr_store(b, _):
        i0 = pl.multiple_of(b * BLK, BLK)
        gn_out[pl.ds(i0, BLK), :] = (scale * narr_acc[pl.ds(i0 + PAD, BLK), :]).astype(BF16)
        return 0

    lax.fori_loop(0, blocks, narr_store, 0)
    narr_out = pltpu.make_async_copy(gn_out, gn_hbm, out_sem.at[1])
    narr_out.start()

    for c in range(max(0, ZC - LAG), ZC):
        take_down(c)

    @pl.when(has_next)
    def _():
        halo_next().wait_send()
        edge_next().wait_send()

    @pl.when(has_prev)
    def _():
        halo_prev().wait_send()
        edge_prev().wait_send()

    for k in range(1, Q):
        stat_copy(k).wait_send()
    for k in range(chips):
        pair_copy(k).wait_send()
    for k in range(1, chips):
        chip_copy(k).wait_send()

    def drain(c, _):
        @pl.when(t < root)
        def _():
            up_right(c).wait_send()

        @pl.when(t > root)
        def _():
            up_left(c).wait_send()

        @pl.when(left_child)
        def _():
            down_left(c).wait_send()

        @pl.when(right_child)
        def _():
            down_right(c).wait_send()

        store_queue(c).wait()
        return 0

    lax.fori_loop(0, ZC, drain, 0)
    clips_store.wait()
    narr_out.wait()


def shards(T, Q, clips, narrations, queue, loss_weights, offsets, valid):
    rows, width = clips.shape
    negs = queue.shape[0]
    chips = Q // 2
    own = rows // Q
    zc = 8
    vmem = pl.BlockSpec(memory_space=pltpu.VMEM)
    hbm = pl.BlockSpec(memory_space=pl.ANY)
    dma = pltpu.SemaphoreType.DMA
    return pl.pallas_call(
        functools.partial(kernel, T, Q, zc),
        out_shape=(
            jax.ShapeDtypeStruct((own, width), BF16),
            jax.ShapeDtypeStruct((rows, width), BF16),
            jax.ShapeDtypeStruct((negs, width), BF16),
        ),
        in_specs=[vmem, hbm, vmem, vmem, vmem, vmem],
        out_specs=(hbm, hbm, hbm),
        scratch_shapes=[
            pltpu.VMEM((rows + 2 * PAD, width), BF16),
            pltpu.VMEM((negs, rows), F32),
            pltpu.VMEM((negs, rows), BF16),
            pltpu.VMEM((Q, 2, rows), F32),
            pltpu.VMEM((16, rows), F32),
            pltpu.VMEM((16, rows), F32),
            pltpu.VMEM((16, rows), F32),
            pltpu.VMEM((rows + 2 * PAD, width), F32),
            pltpu.VMEM((2, PAD, width), F32),
            pltpu.VMEM((negs, width), F32),
            pltpu.VMEM((negs, width), BF16),
            pltpu.VMEM((2, negs, width), BF16),
            pltpu.VMEM((negs, width), BF16),
            pltpu.VMEM((rows, width), F32),
            pltpu.VMEM((rows, width), BF16),
            pltpu.VMEM((chips, own, width), BF16),
            pltpu.VMEM((chips, own, width), BF16),
            pltpu.VMEM((chips, own, width), BF16),
            pltpu.VMEM((rows, width), F32),
            pltpu.VMEM((own, width), BF16),
            pltpu.VMEM((rows, width), BF16),
            dma, dma((2,)), dma((2,)), dma((Q,)), dma((Q,)),
            dma((zc,)), dma((2, zc)), dma((2, zc)), dma((zc,)),
            dma((chips,)), dma((chips,)), dma((chips,)), dma((chips,)),
            dma((2,)), dma((2,)), dma((zc,)), dma((2,)),
        ],
        compiler_params=pltpu.CompilerParams(
            collective_id=0, has_side_effects=True, vmem_limit_bytes=60 * 1024 * 1024),
        cost_estimate=pl.CostEstimate(
            flops=6 * rows * negs * width, bytes_accessed=8 * rows * width, transcendentals=rows * negs),
        name="mil_nce_grad",
    )(clips, narrations, queue, loss_weights[None, :], offsets.T, valid.T)


def solution(mesh):
    placed = (P("tm", None), P("tm", None), P("queue", None), P("tm"), P("tm", None), P("tm", None))
    return jax.shard_map(
        functools.partial(shards, mesh.shape["tm"], mesh.shape["queue"]),
        mesh=mesh,
        in_specs=placed,
        out_specs=(P(("tm", "queue"), None), P("tm", None), P("queue", None)),
        check_vma=False,
    )
```

time: 259 us -> 68.4 us (0.26); the launches traced: 256 us -> 68.2 us
  waiting for transfers between devices: 90 us -> 0 us
  other arithmetic: 72.4 us -> 0 us
  Pallas kernels: 0 us -> 61.8 us
  blocking collectives: 25.8 us -> 0 us
  matrix products: 22.6 us -> 0 us
  local copies, waits for them, and re-layouts: 21.3 us -> 5.78 us
  between operations: 14.3 us -> 0.64 us
  starting transfers between devices: 9.53 us -> 0 us
    psum x2 -> x0, waiting for transfers between devices: 89.9 us -> none  [the longest x1 82.7 us: shards(): lax.psum(jnp.dot(neg_coef, queue, preferred_element_type=jnp.float32), 'q...]
    pallas_call x0 -> x1, Pallas kernels: none -> 61.8 us  [shards(): pl.pallas_call(functools.partial(kernel, T, Q, zc), out_shape=(jax.ShapeD...]
    dot_general x3 -> x0, matrix products: 22.6 us -> none  [the longest x1 7.78 us: shards(): jnp.dot(neg_coef, queue, preferred_element_type=jnp.float32)]
    mul x11 -> x0, other arithmetic: 19 us -> none  [the longest x1 18.8 us: shards(): coef * clips]
    add x4 -> x0, other arithmetic: 13.9 us -> none  [the longest x1 12.4 us: shards(): narr_grad + jnp.pad(coef * clips, ((HALO + delta, HALO - delta), (0, 0)))]
    pmax x1 -> x0, blocking collectives: 13.6 us -> none  [shards(): shift = lax.pmax(local_top, 'queue')]
    concatenate x2 -> x0, local copies, waits for them, and re-layouts: 13.4 us -> none  [the longest x1 13.4 us: shards(): jnp.concatenate([middle[:HALO] + from_prev, middle[HALO:rows - HALO], mid...]
    dot_general x1 -> x0, other arithmetic: 12.5 us -> none  [shards(): jnp.einsum('ie,ie->i', clips, piece, preferred_element_type=jnp.float32)]
  transfers between devices with their start and end apart: 6 -> 0, of which waited for: 2 -> 0; matrix products, arithmetic and copies ran while one was open for 33% -> 0% of each run, Pallas kernels for 0% -> 0%
where the time goes in v1:
time: 68.4 us; the launch traced here: 68.2 us
  Pallas kernels  61.8 us (90%)
  local copies, waits for them, and re-layouts  5.78 us (8%)
    pallas_call x1, Pallas kernels, shards(): pl.pallas_call(functools.partial(kernel, T, Q, zc), out_shape=(jax.ShapeD...  61.8 us
    unnamed x5, local copies, waits for them, and re-layouts  5.78 us

profile of v1, /device:TPU:24, one launch (start us, length us, event | category | flops | bytes accessed | tf_op | source)
XLA Modules:
  0.0 68.2 jit_solution(5058017045867939458)
XLA Ops:
  0.6 61.8 %mil_nce_grad.1 = (bf16[256,512]{1,0:T(8,128)(2,1)}, bf16[2048,512]{1,0:T(8,128)(2,1)}, bf16[1024,512]{1,0:T(8,128)(2,1)}) custom-call(bf16[2048,512]{1,0:T(8,128)(2,1)} %clips.1, bf16[2048,512]{1,0:T(8,128)(2,1)} %narr_hbm.1, bf16[1024,512]{1,0:T(8,128)(2,1)} %queue.1, f32[1,2048]{1,0:T(1,128)} %bitcast.5, s32[8,2048]{1,0:T(8,128)} %bitcast.3, ...), custom_call_target="tpu_custom_call" | custom-call | flops 6442450944 | bytes 8388608 | tf_op jit(solution)/shard_map/mil_nce_grad/pallas_call | solution.py:428
  62.4 1.7 %copy.12 = bf16[256,512]{1,0:T(8,128)(2,1)} copy(bf16[256,512]{1,0:T(8,128)(2,1)} %get-tuple-element.6) | data formatting | bytes 524288
  64.1 0.0 copy-start
  64.1 3.1 %copy.13 = bf16[2048,512]{1,0:T(8,128)(2,1)} copy(bf16[2048,512]{1,0:T(8,128)(2,1)} %get-tuple-element.7) | data formatting | bytes 4194304
  67.2 0.0 copy-done
  67.2 1.0 %copy.14 = bf16[1024,512]{1,0:T(8,128)(2,1)} copy(bf16[1024,512]{1,0:T(8,128)(2,1)S(1)} %copy-done) | data formatting | bytes 2097152
Async XLA Ops:
  64.1 3.1 %copy-start = (bf16[1024,512]{1,0:T(8,128)(2,1)S(1)}, bf16[1024,512]{1,0:T(8,128)(2,1)}, u32[]{:S(2)}) copy-start(bf16[1024,512]{1,0:T(8,128)(2,1)} %get-tuple-element.8) | copy-start | bytes 3145732

commit v2 on v1

--- a/solution.py
+++ b/solution.py
@@ -12,7 +12,8 @@
 PAD = 16
 BLK = 128
 WIN = BLK + 2 * PAD
-LAG = 2
+LAG = 4
+SUB = 2
 MESH = pl.DeviceIdType.MESH
 F32 = jnp.float32
 BF16 = jnp.bfloat16
@@ -24,17 +25,19 @@
     return lax.dot_general(a, b, dims, preferred_element_type=F32)
 
 
-def kernel(T, Q, ZC, clips, narr_hbm, queue, weights, offsets, valid, gc_hbm, gn_hbm, gq_hbm,
-           ext, scores, coef, stat, bag_s, counts, bag_c, narr_acc, edge, part, up_tx, up_rx, fin,
-           grad_f, grad_b, pair_rx, chip_tx, chip_rx, bag_grad, gc_out, gn_out,
+def kernel(T, Q, ZC, clips, narr_hbm, queue, weights, offsets, valid, gc_out, gn_out, fin,
+           ext, scores, coef, stat, bag_s, counts, bag_c, narr_acc, edge, part, up_tx, up_rx,
+           grad_f, grad_b, pair_rx, chip_tx, chip_rx, bag_grad,
            load_sem, halo_ss, halo_rs, stat_ss, stat_rs, up_ss, up_rs, down_ss, down_rs,
-           pair_ss, pair_rs, chip_ss, chip_rs, edge_ss, edge_rs, gq_sem, out_sem):
+           pair_ss, pair_rs, chip_ss, chip_rs, edge_ss, edge_rs):
     rows, width = clips.shape
     negs = queue.shape[0]
     scale = 0.75 / math.sqrt(width)
     chips = Q // 2
     own = rows // Q
     zn = negs // ZC
+    qn = zn * SUB
+    steps = ZC // SUB
     blocks = rows // BLK
     root = (T - 1) // 2
     t = lax.axis_index("tm")
@@ -190,9 +193,6 @@
     def down_right(c):
         return remote(fin.at[zrows(c)], fin.at[zrows(c)], down_ss.at[1, c], down_rs.at[c], (t + 1, q))
 
-    def store_queue(c):
-        return pltpu.make_async_copy(fin.at[zrows(c)], gq_hbm.at[zrows(c)], gq_sem.at[c])
-
     def pass_down(c):
         @pl.when(left_child)
         def _():
@@ -202,8 +202,6 @@
         def _():
             down_right(c).start()
 
-        store_queue(c).start()
-
     def send_up(c):
         up_tx[zrows(c), :] = part[zrows(c), :].astype(BF16)
 
@@ -216,17 +214,17 @@
             up_left(c).start()
 
     def queue_part(c, _):
-        p = (scores[zrows(c), :] * factor).astype(BF16)
-        coef[zrows(c), :] = p
-        part[zrows(c), :] = dot(p, clips[...])
+        r = pl.ds(pl.multiple_of(c * qn, qn), qn)
+        p = (scores[r, :] * factor).astype(BF16)
+        coef[r, :] = p
+        part[r, :] = dot(p, clips[...])
 
         @pl.when(leaf)
         def _():
-            send_up(c)
-
-        return 0
-
-    lax.fori_loop(0, ZC, queue_part, 0)
+            for j in range(SUB):
+                send_up(c * SUB + j)
+
+        return 0
 
     def gather_up(c):
         @pl.when(left_child)
@@ -261,15 +259,12 @@
         return remote(grad_b.at[own_rows(2 * p + 1 - core)], pair_rx.at[p],
                       pair_ss.at[p], pair_rs.at[p], (t, q + 1 - 2 * core))
 
-    def pair_part(p, _):
+    def pair_part(p):
         r = pl.ds(pl.multiple_of(p * 2 * own, 2 * own), 2 * own)
         g = dot(coef[:, r], queue[...], TN)
         grad_f[r, :] = g
         grad_b[r, :] = g.astype(BF16)
         pair_copy(p).start()
-        return 0
-
-    lax.fori_loop(0, chips, pair_part, 0)
 
     def chip_copy(k):
         peer = lax.rem(chip + k, chips)
@@ -302,31 +297,33 @@
         def _():
             bag_grad[pl.ds(i0, BLK), :] = dot(band, ext[pl.ds(i0, WIN), :], TN)
 
-    chip_steps = -(-(chips - 1) // ZC)
+    middle = (left_child | right_child) & (t != root)
+    chip_from = ZC // 4 + 1
+    pair_steps = -(-chips // (ZC // 4))
+    chip_steps = -(-(chips - 1) // (ZC - chip_from))
     narr_steps = -(-blocks // ZC)
+
+    def guarded(index, start, stop, work):
+        @pl.when((index >= start) & (index < stop))
+        def _():
+            work(index)
 
     def mixed(c, _):
         gather_up(c)
+
+        @pl.when(middle & (c >= LAG))
+        def _():
+            take_down(c - LAG)
+
+        for j in range(pair_steps):
+            guarded(c * pair_steps + j, 0, chips, pair_part)
         for j in range(chip_steps):
-            k = c * chip_steps + j + 1
-
-            @pl.when(k < chips)
-            def _():
-                chip_part(k)
-
+            guarded((c - chip_from) * chip_steps + j + 1, 1, chips, chip_part)
         for j in range(narr_steps):
-            b = c * narr_steps + j
-
-            @pl.when(b < blocks)
-            def _():
-                narr_part(b)
-
-        @pl.when(c >= LAG)
-        def _():
-            take_down(c - LAG)
-
-        return 0
-
+            guarded(c * narr_steps + j, 0, blocks, narr_part)
+        return 0
+
+    lax.fori_loop(0, steps, queue_part, 0)
     lax.fori_loop(0, ZC, mixed, 0)
 
     def edge_next():
@@ -349,8 +346,6 @@
         chip_copy(k).wait_recv()
         g = g + chip_rx[k].astype(F32)
     gc_out[...] = (scale * g).astype(BF16)
-    clips_store = pltpu.make_async_copy(gc_out, gc_hbm, out_sem.at[0])
-    clips_store.start()
 
     @pl.when(has_prev)
     def _():
@@ -368,11 +363,19 @@
         return 0
 
     lax.fori_loop(0, blocks, narr_store, 0)
-    narr_out = pltpu.make_async_copy(gn_out, gn_hbm, out_sem.at[1])
-    narr_out.start()
 
     for c in range(max(0, ZC - LAG), ZC):
+        @pl.when(middle)
+        def _():
+            take_down(c)
+
+    def last_down(c, _):
         take_down(c)
+        return 0
+
+    @pl.when(leaf)
+    def _():
+        lax.fori_loop(0, ZC, last_down, 0)
 
     @pl.when(has_next)
     def _():
@@ -408,12 +411,18 @@
         def _():
             down_right(c).wait_send()
 
-        store_queue(c).wait()
         return 0
 
     lax.fori_loop(0, ZC, drain, 0)
-    clips_store.wait()
-    narr_out.wait()
+
+
+def store_kernel(*refs):
+    sources, targets, sem = refs[:3], refs[3:6], refs[6]
+    copies = [pltpu.make_async_copy(sources[k], targets[k], sem.at[k]) for k in range(3)]
+    for copy in copies:
+        copy.start()
+    for copy in copies:
+        copy.wait()
 
 
 def shards(T, Q, clips, narrations, queue, loss_weights, offsets, valid):
@@ -421,19 +430,19 @@
     negs = queue.shape[0]
     chips = Q // 2
     own = rows // Q
-    zc = 8
+    zc = 16
     vmem = pl.BlockSpec(memory_space=pltpu.VMEM)
     hbm = pl.BlockSpec(memory_space=pl.ANY)
     dma = pltpu.SemaphoreType.DMA
-    return pl.pallas_call(
+    grads = pl.pallas_call(
         functools.partial(kernel, T, Q, zc),
         out_shape=(
-            jax.ShapeDtypeStruct((own, width), BF16),
-            jax.ShapeDtypeStruct((rows, width), BF16),
-            jax.ShapeDtypeStruct((negs, width), BF16),
+            pltpu.VMEM((own, width), BF16),
+            pltpu.VMEM((rows, width), BF16),
+            pltpu.VMEM((negs, width), BF16),
         ),
         in_specs=[vmem, hbm, vmem, vmem, vmem, vmem],
-        out_specs=(hbm, hbm, hbm),
+        out_specs=(vmem, vmem, vmem),
         scratch_shapes=[
             pltpu.VMEM((rows + 2 * PAD, width), BF16),
             pltpu.VMEM((negs, rows), F32),
@@ -447,26 +456,31 @@
             pltpu.VMEM((negs, width), F32),
             pltpu.VMEM((negs, width), BF16),
             pltpu.VMEM((2, negs, width), BF16),
-            pltpu.VMEM((negs, width), BF16),
             pltpu.VMEM((rows, width), F32),
             pltpu.VMEM((rows, width), BF16),
             pltpu.VMEM((chips, own, width), BF16),
             pltpu.VMEM((chips, own, width), BF16),
             pltpu.VMEM((chips, own, width), BF16),
             pltpu.VMEM((rows, width), F32),
-            pltpu.VMEM((own, width), BF16),
-            pltpu.VMEM((rows, width), BF16),
             dma, dma((2,)), dma((2,)), dma((Q,)), dma((Q,)),
             dma((zc,)), dma((2, zc)), dma((2, zc)), dma((zc,)),
             dma((chips,)), dma((chips,)), dma((chips,)), dma((chips,)),
-            dma((2,)), dma((2,)), dma((zc,)), dma((2,)),
+            dma((2,)), dma((2,)),
         ],
         compiler_params=pltpu.CompilerParams(
-            collective_id=0, has_side_effects=True, vmem_limit_bytes=60 * 1024 * 1024),
+            collective_id=0, has_side_effects=True, vmem_limit_bytes=52 * 1024 * 1024),
         cost_estimate=pl.CostEstimate(
             flops=6 * rows * negs * width, bytes_accessed=8 * rows * width, transcendentals=rows * negs),
         name="mil_nce_grad",
     )(clips, narrations, queue, loss_weights[None, :], offsets.T, valid.T)
+    return pl.pallas_call(
+        store_kernel,
+        out_shape=tuple(jax.ShapeDtypeStruct(g.shape, g.dtype) for g in grads),
+        in_specs=[vmem] * 3,
+        out_specs=(hbm,) * 3,
+        scratch_shapes=[dma((3,))],
+        name="store_grads",
+    )(*[pltpu.with_memory_space_constraint(g, pltpu.VMEM) for g in grads])
 
 
 def solution(mesh):

time: 68.4 us -> 56.7 us (0.83)
  Pallas kernels: 61.8 us -> 55.6 us
  local copies, waits for them, and re-layouts: 5.78 us -> 0 us
    pallas_call x1 -> x2, Pallas kernels: 61.8 us -> 55.6 us  [the longest x1 53.8 us: shards(): pl.pallas_call(functools.partial(kernel, T, Q, zc), out_shape=(pltpu.VMEM...]
    unnamed x5 -> x0, local copies, waits for them, and re-layouts: 5.78 us -> none
where the time goes in v2:
time: 56.7 us; the launch traced here: 56.2 us
  Pallas kernels  55.6 us (98%)
  between operations  0.64 us (1%)
    pallas_call x1, Pallas kernels, shards(): pl.pallas_call(functools.partial(kernel, T, Q, zc), out_shape=(pltpu.VMEM...  53.8 us
    pallas_call x1, Pallas kernels, shards(): pl.pallas_call(store_kernel, out_shape=tuple((jax.ShapeDtypeStruct(g.shap...  1.77 us

profile of v2, /device:TPU:24, one launch (start us, length us, event | category | flops | bytes accessed | tf_op | source)
XLA Modules:
  0.0 56.2 jit_solution(15579840361635325276)
XLA Ops:
  0.6 53.8 %mil_nce_grad.1 = (bf16[256,512]{1,0:T(8,128)(2,1)S(1)}, bf16[2048,512]{1,0:T(8,128)(2,1)S(1)}, bf16[1024,512]{1,0:T(8,128)(2,1)S(1)}) custom-call(bf16[2048,512]{1,0:T(8,128)(2,1)} %clips.1, bf16[2048,512]{1,0:T(8,128)(2,1)} %narr_hbm.1, bf16[1024,512]{1,0:T(8,128)(2,1)} %queue.1, f32[1,2048]{1,0:T(1,128)} %bitcast.5, s32[8,2048]{1,0:T(8,128)} %bitcast.3, ...), custom_call_target="tpu_custom_call" | custom-call | flops 6442450944 | bytes 8388608 | tf_op jit(solution)/shard_map/mil_nce_grad/pallas_call | solution.py:437
  54.5 1.8 %store_grads.1 = (bf16[256,512]{1,0:T(8,128)(2,1)}, bf16[2048,512]{1,0:T(8,128)(2,1)}, bf16[1024,512]{1,0:T(8,128)(2,1)}) custom-call(bf16[256,512]{1,0:T(8,128)(2,1)S(1)} %get-tuple-element.6.refs_0_, bf16[2048,512]{1,0:T(8,128)(2,1)S(1)} %get-tuple-element.7.refs_1_, bf16[1024,512]{1,0:T(8,128)(2,1)S(1)} %get-tuple-element.8.refs_2_), custom_call_target="tpu_custom_call" | custom-call | tf_op jit(solution)/shard_map/store_grads/pallas_call | solution.py:476
